TPU v7x, 32 devices: a whole 2x2x4 slice. The times are simulated.
32 devices in a mesh: ctx: 1, exp: 16 (over z, y, x), rep: 2 (over core).
Axes of the slice: x: 2, y: 2, z: 4, core: 2. Of those that a mesh axis runs over, the one named last changes fastest.
Arguments:
- hidden_in: bfloat16 [1024, 4096], P(('rep', 'ctx', 'exp')), parts along dimension 0, may hold values from -6 to 6
- queries: bfloat16 [1024, 8192], P(('rep', 'ctx'), 'exp'), parts along dimension 0, may hold values from -64 to 64
- keys: bfloat16 [1024, 512], P(('rep', 'ctx')), parts along dimension 0, may hold values from -8 to 8
- values: bfloat16 [1024, 512], P(('rep', 'ctx')), parts along dimension 0, may hold values from -6 to 6
- out_proj: bfloat16 [8192, 4096], P('exp'), may hold values from -0.0625 to 0.0625
- norm_gain: float32 [4096], replicated, may hold values from 0.1 to 1.9
- expert_ids: int32 [1024, 8], P(('rep', 'ctx', 'exp')), parts along dimension 0, may hold values from 0 to 127, all different within a row; in each aligned block of 32 rows (0 to 31, 32 to 63, ...) at most 2 rows name the same one
- gate_fixed: int32 [1024, 8], P(('rep', 'ctx', 'exp')), parts along dimension 0, may hold values from 1 to 4096
- live_counts: int32 [32], P(('rep', 'ctx', 'exp')), parts along dimension 0, may hold values from 16 to 32, as said below
- gate_proj: bfloat16 [16, 4096, 1536], P('exp', None, 'ctx'), may hold values from -0.09375 to 0.09375
- up_proj: bfloat16 [16, 4096, 1536], P('exp', None, 'ctx'), may hold values from -0.09375 to 0.09375
- down_proj: bfloat16 [16, 1536, 4096], P('exp', 'ctx'), may hold values from -0.4375 to 0.4375
Outputs:
- mixed: bfloat16 [1024, 4096], P(('rep', 'ctx', 'exp')), parts along dimension 0
- expert_sum: bfloat16 [1024, 4096], P(('rep', 'ctx', 'exp')), parts along dimension 0
There are 2 independent parts, one for each index of `rep`. A program takes and returns all parts, laid end to end along the dimension named above; an argument that names none is the same for every part. Nothing has to cross between parts.
Inputs may be any that keep to these rules, and one draw needn't show every extreme that they name: `expert_ids`: each row names 8 different experts; among the 32 rows of one device no expert is named by more than 2 rows. `live_counts`: some device has all of its rows live.
All inputs are finite; a program needn't handle non-finite values.
Results may differ from a plain program's by a relative error of at most 0.023.
Values may be sent and summed in bfloat16 or wider, within the bound.
A program may use at most 128 MiB of HBM per device.

v0:
```python
import jax
import jax.numpy as jnp
from jax import lax
from jax.experimental import pallas as pl
from jax.experimental.pallas import tpu as pltpu
from jax.sharding import PartitionSpec as P

D = 4096
HEADS = 64
KV_HEADS = 4
HEAD_DIM = 128
TOPK = 8
CAP = 2


N_EXP = 16
ROWS = 32
SEQ = N_EXP * ROWS
HEAD_COLS = 512
FF = 1536
WIDE = 512
CHUNKS = D // WIDE
SLOTS = N_EXP * CAP
QBLOCK = 256
PIECES = 8
PAIR = 2 * WIDE
HALVES = 2


def fused_kernel(
    hidden_ref,
    q_ref,
    k_ref,
    v_ref,
    gain_ref,
    ids_ref,
    fixed_ref,
    live_ref,
    proj_hbm,
    gate_hbm,
    up_hbm,
    down_hbm,
    mixed_ref,
    sum_ref,
    proj,
    gate,
    up,
    down,
    attended,
    part,
    got1,
    got2,
    got3,
    gate_sum,
    up_sum,
    hid,
    send_rows,
    got_rows,
    send_back,
    got_back,
    send_norm,
    got_norm,
    load_sem,
    send1,
    recv1,
    send2,
    recv2,
    send3,
    recv3,
    send4,
    recv4,
    send5,
    recv5,
    send6,
    recv6,
):
    me = lax.axis_index("exp")
    x, y, z = me % 2, (me // 2) % 2, me // 4
    loads = [
        pltpu.make_async_copy(source, target, load_sem.at[i])
        for i, (source, target) in enumerate(
            [(proj_hbm, proj), (gate_hbm.at[0], gate), (up_hbm.at[0], up), (down_hbm.at[0], down)]
        )
    ]
    for load in loads:
        load.start()

    barrier = pltpu.get_barrier_semaphore()
    for step in range(1, N_EXP):
        pl.semaphore_signal(
            barrier,
            inc=1,
            device_id={"exp": (me + step) % N_EXP},
            device_id_type=pl.DeviceIdType.MESH,
        )

    kv = (me * (HEAD_COLS // HEAD_DIM)) // (HEADS // KV_HEADS)
    kv_cols = pl.ds(pl.multiple_of(kv * HEAD_DIM, HEAD_DIM), HEAD_DIM)
    scale = HEAD_DIM ** (-0.5)
    for block in range(SEQ // QBLOCK):
        first = block * QBLOCK
        keys_seen = first + QBLOCK
        q_pos = first + lax.broadcasted_iota(jnp.int32, (QBLOCK, keys_seen), 0)
        k_pos = lax.broadcasted_iota(jnp.int32, (QBLOCK, keys_seen), 1)
        visible = k_pos <= q_pos
        for head in range(HEAD_COLS // HEAD_DIM):
            cols = slice(head * HEAD_DIM, (head + 1) * HEAD_DIM)
            scores = (
                lax.dot_general(
                    q_ref[first : first + QBLOCK, cols],
                    k_ref[:keys_seen, kv_cols],
                    (((1,), (1,)), ((), ())),
                    preferred_element_type=jnp.float32,
                )
                * scale
            )
            scores = jnp.where(visible, scores, -1e30)
            largest = jnp.max(scores, axis=1, keepdims=True)
            weights = jnp.exp(scores - largest)
            total = jnp.sum(weights, axis=1, keepdims=True)
            summed = jnp.dot(
                weights.astype(jnp.bfloat16),
                v_ref[:keys_seen, kv_cols],
                preferred_element_type=jnp.float32,
            )
            attended[first : first + QBLOCK, cols] = (summed / total).astype(jnp.bfloat16)

    loads[0].wait()
    pl.semaphore_wait(barrier, N_EXP - 1)

    x_peer, y_peer = me + 1 - 2 * x, me + 2 - 4 * y

    def places(odd):
        return (y, x, y_peer, x_peer) if odd else (x, y, x_peer, y_peer)

    def copy1(chunk, odd):
        a, _, peer, _ = places(odd)
        return pltpu.make_async_remote_copy(
            src_ref=part.at[chunk, 1 - a],
            dst_ref=got1.at[chunk],
            send_sem=send1.at[chunk],
            recv_sem=recv1.at[chunk],
            device_id={"exp": peer},
            device_id_type=pl.DeviceIdType.MESH,
        )

    def copy2(chunk, odd):
        a, b, _, peer = places(odd)
        return pltpu.make_async_remote_copy(
            src_ref=part.at[chunk, a, 1 - b],
            dst_ref=got2.at[chunk],
            send_sem=send2.at[chunk],
            recv_sem=recv2.at[chunk],
            device_id={"exp": peer},
            device_id_type=pl.DeviceIdType.MESH,
        )

    def copy3(chunk, odd, step):
        a, b, _, _ = places(odd)
        other = (z + step) % 4
        return pltpu.make_async_remote_copy(
            src_ref=part.at[chunk, a, b, other],
            dst_ref=got3.at[chunk, step - 1],
            send_sem=send3.at[chunk, step - 1],
            recv_sem=recv3.at[chunk, step - 1],
            device_id={"exp": me + (other - z) * 4},
            device_id_type=pl.DeviceIdType.MESH,
        )

    def project(pair):
        for odd in (0, 1):
            chunk = pair * 2 + odd
            cols = slice(chunk * WIDE, (chunk + 1) * WIDE)
            for half in range(2):
                lines = SEQ // 2
                product = jnp.dot(
                    attended[half * lines : (half + 1) * lines, :],
                    proj[:, cols],
                    preferred_element_type=jnp.float32,
                ).astype(jnp.bfloat16)
                for local in range(N_EXP // 2):
                    owner = half * (N_EXP // 2) + local
                    ox, oy, oz = owner % 2, (owner // 2) % 2, owner // 4
                    a, b = (oy, ox) if odd else (ox, oy)
                    part[chunk, a, b, oz] = product[local * ROWS : (local + 1) * ROWS, :]
            copy1(chunk, odd).start()

    def fold1(pair):
        for odd in (0, 1):
            chunk = pair * 2 + odd
            a = places(odd)[0]
            copy1(chunk, odd).wait_recv()
            for b in range(2):
                for c in range(4):
                    part[chunk, a, b, c] = part[chunk, a, b, c] + got1[chunk, b, c]
            copy2(chunk, odd).start()

    def fold2(pair):
        for odd in (0, 1):
            chunk = pair * 2 + odd
            a, b, _, _ = places(odd)
            copy2(chunk, odd).wait_recv()
            for c in range(4):
                part[chunk, a, b, c] = part[chunk, a, b, c] + got2[chunk, c]
            for step in range(1, 4):
                copy3(chunk, odd, step).start()

    project(0)
    project(1)

    slot = lax.broadcasted_iota(jnp.int32, (SLOTS, ROWS), 0)
    row = lax.broadcasted_iota(jnp.int32, (SLOTS, ROWS), 1)
    weight = jnp.zeros((SLOTS, ROWS), jnp.int32)
    named = jnp.zeros((SLOTS, ROWS), jnp.float32)
    for k in range(TOPK):
        same = (ids_ref[k : k + 1, :] == slot // CAP) & (row < live_ref[0])
        weight = weight + jnp.where(same, fixed_ref[k : k + 1, :], 0)
        named = named + jnp.where(same, 1.0, 0.0)
    before = lax.broadcasted_iota(jnp.int32, (ROWS, ROWS), 0) < lax.broadcasted_iota(
        jnp.int32, (ROWS, ROWS), 1
    )
    earlier = jnp.dot(
        named.astype(jnp.bfloat16),
        jnp.where(before, 1.0, 0.0).astype(jnp.bfloat16),
        preferred_element_type=jnp.float32,
    )
    taken = (named > 0.5) & (jnp.abs(earlier - (slot % CAP).astype(jnp.float32)) < 0.5)
    dispatch_exact = jnp.where(taken, 1.0, 0.0)
    dispatch = dispatch_exact.astype(jnp.bfloat16)
    weight = jnp.where(taken, weight, 0)
    coarse = (weight // 64) * 64
    combine_hi = (coarse.astype(jnp.float32) / 4096.0).astype(jnp.bfloat16)
    combine_lo = ((weight - coarse).astype(jnp.float32) / 4096.0).astype(jnp.bfloat16)

    lines = SLOTS * PIECES
    per = CAP * PIECES
    i = lax.broadcasted_iota(jnp.int32, (lines, lines), 0)
    j = lax.broadcasted_iota(jnp.int32, (lines, lines), 1)
    to_work = jnp.where((i % SLOTS) * PIECES + i // SLOTS == j, 1.0, 0.0).astype(jnp.bfloat16)
    to_travel = jnp.where((j % SLOTS) * PIECES + j // SLOTS == i, 1.0, 0.0).astype(jnp.bfloat16)

    def reorder(matrix, value):
        return jnp.dot(matrix, value, preferred_element_type=jnp.float32).astype(jnp.bfloat16)

    def pieces_of(value):
        width = value.shape[1] // PIECES
        return jnp.concatenate(
            [value[:, p * width : (p + 1) * width] for p in range(PIECES)], axis=0
        )

    def whole_of(value):
        return jnp.concatenate(
            [value[p * SLOTS : (p + 1) * SLOTS, :] for p in range(PIECES)], axis=1
        )

    def exchange(source, target, send_sem, recv_sem, part_index, step):
        other = (me + step) % N_EXP
        return pltpu.make_async_remote_copy(
            src_ref=source.at[part_index, other],
            dst_ref=target.at[part_index, me],
            send_sem=send_sem.at[part_index, step - 1],
            recv_sem=recv_sem.at[part_index, step - 1],
            device_id={"exp": other},
            device_id_type=pl.DeviceIdType.MESH,
        )

    def there(pair, step):
        return exchange(send_rows, got_rows, send4, recv4, pair, step)

    def back(half, step):
        return exchange(send_back, got_back, send5, recv5, half, step)

    def norms(step):
        return exchange(send_norm, got_norm, send6, recv6, 0, step)

    def each_step(action):
        def body(step, _):
            action(step)
            return 0

        lax.fori_loop(1, N_EXP, body, 0)

    squares = [jnp.zeros((ROWS, 1), jnp.float32)]

    def final(pair):
        picked = []
        for odd in (0, 1):
            chunk = pair * 2 + odd
            a, b, _, _ = places(odd)
            for step in range(1, 4):
                copy3(chunk, odd, step).wait_recv()
            cols = slice(chunk * WIDE, (chunk + 1) * WIDE)
            total = part[chunk, a, b, z].astype(jnp.float32)
            for step in range(3):
                total = total + got3[chunk, step].astype(jnp.float32)
            total = total + hidden_ref[:, cols].astype(jnp.float32)
            mixed_ref[:, cols] = total.astype(jnp.bfloat16)
            squares[0] = squares[0] + jnp.sum(total * total, axis=1, keepdims=True)
            gained = (total * gain_ref[:, cols]).astype(jnp.bfloat16)
            picked.append(reorder(dispatch, gained))
        ordered = reorder(to_travel, pieces_of(jnp.concatenate(picked, axis=1)))
        for e in range(N_EXP):
            send_rows[pair, e] = ordered[e * per : (e + 1) * per, :]
        each_step(lambda step: there(pair, step).start())
        got_rows[pair, me] = send_rows[pair, me]

    def send_norms():
        norm = lax.rsqrt(squares[0] / D + 1e-06)
        wide = jnp.broadcast_to(norm, (ROWS, 128))
        slot_norm = jnp.dot(
            dispatch_exact, wide, precision=lax.Precision.HIGHEST, preferred_element_type=jnp.float32
        )
        line = lax.broadcasted_iota(jnp.int32, (N_EXP * 8, SLOTS), 0)
        source = lax.broadcasted_iota(jnp.int32, (N_EXP * 8, SLOTS), 1)
        spread = jnp.where((line // 8) * CAP + line % CAP == source, 1.0, 0.0)
        tiles = jnp.dot(
            spread, slot_norm, precision=lax.Precision.HIGHEST, preferred_element_type=jnp.float32
        )
        for e in range(N_EXP):
            send_norm[0, e] = tiles[e * 8 : (e + 1) * 8, :]
        each_step(lambda step: norms(step).start())
        got_norm[0, me] = send_norm[0, me]

    def receive_norms():
        each_step(lambda step: norms(step).wait_recv())
        line = lax.broadcasted_iota(jnp.int32, (SLOTS, N_EXP * 8), 1)
        target = lax.broadcasted_iota(jnp.int32, (SLOTS, N_EXP * 8), 0)
        gather = jnp.where((target // CAP) * 8 + target % CAP == line, 1.0, 0.0)
        return jnp.dot(
            gather,
            got_norm[0].reshape(N_EXP * 8, 128),
            precision=lax.Precision.HIGHEST,
            preferred_element_type=jnp.float32,
        )[:, :1]

    def expert_in(pair):
        if pair == 0:
            for load in loads[1:]:
                load.wait()
        each_step(lambda step: there(pair, step).wait_recv())
        tokens = whole_of(reorder(to_work, got_rows[pair].reshape(lines, PAIR // PIECES)))
        deep = slice(pair * PAIR, (pair + 1) * PAIR)
        for block in range(FF // 512):
            cols = slice(block * 512, (block + 1) * 512)
            for weights_in, sums in ((gate, gate_sum), (up, up_sum)):
                term = jnp.dot(tokens, weights_in[deep, cols], preferred_element_type=jnp.float32)
                sums[:, cols] = term if pair == 0 else sums[:, cols] + term

    fold1(0)
    project(2)
    fold1(1)
    fold2(0)
    project(3)
    fold1(2)
    fold2(1)
    final(0)
    fold1(3)
    fold2(2)
    final(1)
    expert_in(0)
    fold2(3)
    final(2)
    expert_in(1)
    final(3)
    send_norms()
    expert_in(2)
    expert_in(3)
    slot_scale = receive_norms()
    for block in range(FF // 512):
        cols = slice(block * 512, (block + 1) * 512)
        gate_part = gate_sum[:, cols] * slot_scale
        up_part = up_sum[:, cols] * slot_scale
        hid[:, cols] = (gate_part / (1.0 + jnp.exp(-gate_part)) * up_part).astype(jnp.bfloat16)

    width = D // HALVES
    for half in range(HALVES):
        partial_rows = []
        for block in range(width // WIDE):
            first = half * width + block * WIDE
            partial_rows.append(
                jnp.dot(
                    hid[...], down[:, first : first + WIDE], preferred_element_type=jnp.float32
                ).astype(jnp.bfloat16)
            )
        ordered = reorder(to_travel, pieces_of(jnp.concatenate(partial_rows, axis=1)))
        for e in range(N_EXP):
            send_back[half, e] = ordered[e * per : (e + 1) * per, :]
        for step in range(1, N_EXP):
            back(half, step).start()
        got_back[half, me] = send_back[half, me]
    for half in range(HALVES):
        each_step(lambda step: back(half, step).wait_recv())
        returned = whole_of(reorder(to_work, got_back[half].reshape(lines, width // PIECES)))
        over = (((0,), (0,)), ((), ()))
        sum_ref[:, half * width : (half + 1) * width] = (
            lax.dot_general(combine_hi, returned, over, preferred_element_type=jnp.float32)
            + lax.dot_general(combine_lo, returned, over, preferred_element_type=jnp.float32)
        ).astype(jnp.bfloat16)

    def finish(pair, _):
        for odd in (0, 1):
            chunk = pair * 2 + odd
            copy1(chunk, odd).wait_send()
            copy2(chunk, odd).wait_send()
            for step in range(1, 4):
                copy3(chunk, odd, step).wait_send()
        each_step(lambda step: there(pair, step).wait_send())
        return 0

    lax.fori_loop(0, CHUNKS // 2, finish, 0)
    each_step(lambda step: norms(step).wait_send())
    for half in range(HALVES):
        each_step(lambda step: back(half, step).wait_send())


def on_device_fused(
    hidden_in,
    queries,
    keys,
    values,
    out_proj,
    norm_gain,
    expert_ids,
    gate_fixed,
    live_counts,
    gate_proj,
    up_proj,
    down_proj,
):
    bf16 = jnp.bfloat16
    dma = pltpu.SemaphoreType.DMA
    vmem = pl.BlockSpec(memory_space=pltpu.VMEM)
    hbm = pl.BlockSpec(memory_space=pl.ANY)
    going = pltpu.VMEM((D // PAIR, N_EXP, CAP * PIECES, PAIR // PIECES), bf16)
    coming = pltpu.VMEM((HALVES, N_EXP, CAP * PIECES, D // HALVES // PIECES), bf16)
    norm_tiles = pltpu.VMEM((1, N_EXP, 8, 128), jnp.float32)
    return pl.pallas_call(
        fused_kernel,
        out_shape=(jax.ShapeDtypeStruct((ROWS, D), bf16), jax.ShapeDtypeStruct((ROWS, D), bf16)),
        in_specs=[vmem] * 7 + [pl.BlockSpec(memory_space=pltpu.SMEM)] + [hbm] * 4,
        out_specs=(vmem, vmem),
        scratch_shapes=[
            pltpu.VMEM((HEAD_COLS, D), bf16),
            pltpu.VMEM((D, FF), bf16),
            pltpu.VMEM((D, FF), bf16),
            pltpu.VMEM((FF, D), bf16),
            pltpu.VMEM((SEQ, HEAD_COLS), bf16),
            pltpu.VMEM((CHUNKS, 2, 2, 4, ROWS, WIDE), bf16),
            pltpu.VMEM((CHUNKS, 2, 4, ROWS, WIDE), bf16),
            pltpu.VMEM((CHUNKS, 4, ROWS, WIDE), bf16),
            pltpu.VMEM((CHUNKS, 3, ROWS, WIDE), bf16),
            pltpu.VMEM((SLOTS, FF), jnp.float32),
            pltpu.VMEM((SLOTS, FF), jnp.float32),
            pltpu.VMEM((SLOTS, FF), bf16),
            going,
            going,
            coming,
            coming,
            norm_tiles,
            norm_tiles,
            dma((4,)),
            dma((CHUNKS,)),
            dma((CHUNKS,)),
            dma((CHUNKS,)),
            dma((CHUNKS,)),
            dma((CHUNKS, 3)),
            dma((CHUNKS, 3)),
            dma((D // PAIR, N_EXP - 1)),
            dma((D // PAIR, N_EXP - 1)),
            dma((HALVES, N_EXP - 1)),
            dma((HALVES, N_EXP - 1)),
            dma((1, N_EXP - 1)),
            dma((1, N_EXP - 1)),
        ],
        compiler_params=pltpu.CompilerParams(
            collective_id=0, has_side_effects=True, vmem_limit_bytes=56 * 2**20
        ),
        name="decoder_layer",
    )(
        hidden_in,
        queries,
        keys,
        values,
        norm_gain.reshape(1, D),
        expert_ids.T,
        gate_fixed.T,
        live_counts,
        out_proj,
        gate_proj,
        up_proj,
        down_proj,
    )


def on_device_general(
    hidden_in,
    queries,
    keys,
    values,
    out_proj,
    norm_gain,
    expert_ids,
    gate_fixed,
    live_counts,
    gate_proj,
    up_proj,
    down_proj,
):
    n_ctx = lax.axis_size("ctx")
    n_exp = lax.axis_size("exp")
    seq_rows = queries.shape[0]
    local_heads = queries.shape[1] // HEAD_DIM
    group = HEADS // KV_HEADS
    kv_index = lax.axis_index("exp") * local_heads // group
    key_head = lax.dynamic_slice_in_dim(keys, kv_index * HEAD_DIM, HEAD_DIM, 1)
    value_head = lax.dynamic_slice_in_dim(values, kv_index * HEAD_DIM, HEAD_DIM, 1)
    query_heads = queries.reshape(seq_rows, local_heads, HEAD_DIM).transpose(1, 0, 2)
    query_pos = lax.axis_index("ctx") * seq_rows + jnp.arange(seq_rows, dtype=jnp.int32)
    scale = HEAD_DIM ** (-0.5)

    def update(carry, key_block, value_block, first):
        running, total, accum = carry
        scores = (
            jnp.einsum("hqd,kd->hqk", query_heads, key_block, preferred_element_type=jnp.float32)
            * scale
        )
        key_pos = first + jnp.arange(seq_rows, dtype=jnp.int32)
        visible = (key_pos[None, :] <= query_pos[:, None])[None]
        scores = jnp.where(visible, scores, -1e30)
        newest = jnp.maximum(running, jnp.max(scores, axis=2))
        weights = jnp.where(visible, jnp.exp(scores - newest[..., None]), 0.0)
        factor = jnp.exp(running - newest)
        total = total * factor + jnp.sum(weights, axis=2)
        accum = accum * factor[..., None] + jnp.einsum(
            "hqk,kd->hqd",
            weights.astype(jnp.bfloat16),
            value_block,
            preferred_element_type=jnp.float32,
        )
        return (newest, total, accum)

    start_state = (
        jnp.full((local_heads, seq_rows), -1e30, jnp.float32),
        jnp.zeros((local_heads, seq_rows), jnp.float32),
        jnp.zeros((local_heads, seq_rows, HEAD_DIM), jnp.float32),
    )
    carry = start_state
    key_piece = lax.all_gather(key_head, "ctx", axis=0, tiled=True)
    value_piece = lax.all_gather(value_head, "ctx", axis=0, tiled=True)
    blocks = key_piece.shape[0] // seq_rows
    key_blocks = key_piece.reshape(blocks, seq_rows, HEAD_DIM)
    value_blocks = value_piece.reshape(blocks, seq_rows, HEAD_DIM)
    firsts = jnp.arange(blocks, dtype=jnp.int32) * seq_rows

    def step(state, inputs):
        key_block, value_block, first = inputs
        state = update(state, key_block, value_block, first)
        return (state, None)

    carry, _ = lax.scan(step, carry, (key_blocks, value_blocks, firsts))
    running, total, accum = carry
    attended = (
        (accum / total[..., None])
        .astype(jnp.bfloat16)
        .transpose(1, 0, 2)
        .reshape(seq_rows, local_heads * HEAD_DIM)
    )
    token_rows = hidden_in.shape[0]
    attn_out = lax.psum_scatter(
        jnp.dot(attended, out_proj, preferred_element_type=jnp.float32).astype(jnp.bfloat16),
        "exp",
        scatter_dimension=0,
        tiled=True,
    ).astype(jnp.float32)
    residual = hidden_in.astype(jnp.float32) + attn_out
    mixed = residual.astype(jnp.bfloat16)
    norm_scale = lax.rsqrt(jnp.mean(residual * residual, axis=1, keepdims=True) + 1e-06)
    normed = (residual * norm_scale * norm_gain).astype(jnp.bfloat16)
    slot_count = n_exp * CAP
    live = jnp.arange(token_rows, dtype=jnp.int32) < live_counts[0]
    active = (expert_ids < n_exp) & live[:, None]
    onehot = (
        (expert_ids[..., None] == jnp.arange(n_exp, dtype=jnp.int32)) & active[..., None]
    ).astype(jnp.int32)
    onehot = onehot.reshape(token_rows * TOPK, n_exp)
    earlier = jnp.cumsum(onehot, axis=0) - onehot
    rank = jnp.sum(earlier * onehot, axis=1).reshape(token_rows, TOPK)
    slot = jnp.where(active, expert_ids * CAP + rank, -1)
    pair_hit = slot[..., None] == jnp.arange(slot_count, dtype=jnp.int32)
    dispatch = jnp.any(pair_hit, axis=1).astype(jnp.bfloat16)
    send = jnp.einsum("rs,rd->sd", dispatch, normed, preferred_element_type=jnp.float32).astype(
        jnp.bfloat16
    )
    send = send.reshape(n_exp, CAP, D)
    route_weights = gate_fixed.astype(jnp.float32) / 4096.0
    combine = jnp.sum(pair_hit.astype(jnp.float32) * route_weights[..., None], axis=1)
    copies = jnp.broadcast_to(send[None], (n_ctx, n_exp, CAP, D)).reshape(n_ctx * n_exp, CAP, D)
    rows3 = lax.all_to_all(copies, ("ctx", "exp"), split_axis=0, concat_axis=0, tiled=True)
    flat_rows = rows3.reshape(-1, D)
    gate_part = jnp.dot(flat_rows, gate_proj[0], preferred_element_type=jnp.float32)
    up_part = jnp.dot(flat_rows, up_proj[0], preferred_element_type=jnp.float32)
    hidden = (jax.nn.silu(gate_part) * up_part).astype(jnp.bfloat16)
    partial_value = jnp.dot(hidden, down_proj[0], preferred_element_type=jnp.float32)
    partial_value = partial_value.reshape(rows3.shape[0], rows3.shape[1], D).astype(jnp.bfloat16)
    returned = lax.all_to_all(
        partial_value, ("ctx", "exp"), split_axis=0, concat_axis=0, tiled=True
    )
    expert_out = (
        returned.astype(jnp.float32).reshape(n_ctx, slot_count, D).sum(axis=0).astype(jnp.bfloat16)
    )
    expert_sum = jnp.dot(combine, expert_out.astype(jnp.float32), precision=lax.Precision.HIGHEST)
    return (mixed, expert_sum.astype(jnp.bfloat16))


def solution(mesh):
    in_specs = (
        P(("rep", "ctx", "exp"), None),
        P(("rep", "ctx"), "exp"),
        P(("rep", "ctx"), None),
        P(("rep", "ctx"), None),
        P("exp", None),
        P(),
        P(("rep", "ctx", "exp"), None),
        P(("rep", "ctx", "exp"), None),
        P(("rep", "ctx", "exp")),
        P("exp", None, "ctx"),
        P("exp", None, "ctx"),
        P("exp", "ctx", None),
    )
    out_specs = (P(("rep", "ctx", "exp"), None), P(("rep", "ctx", "exp"), None))
    sizes = mesh.shape
    fused = sizes["ctx"] == 1 and sizes["exp"] == N_EXP
    body = on_device_fused if fused else on_device_general
    return jax.shard_map(
        body, mesh=mesh, in_specs=in_specs, out_specs=out_specs, check_vma=False
    )
```

profile of v0, /device:TPU:0, one launch (start us, length us, event | category | flops | bytes accessed | tf_op | source)
XLA Modules:
  0.0 80.7 jit_solution(4958867346264893917)
XLA Ops:
  1.3 76.1 %decoder_layer.1 = (bf16[32,4096]{1,0:T(8,128)(2,1)}, bf16[32,4096]{1,0:T(8,128)(2,1)}) custom-call(bf16[32,4096]{1,0:T(8,128)(2,1)} %hidden_ref.1, bf16[512,512]{1,0:T(8,128)(2,1)} %q_ref.1, bf16[512,512]{1,0:T(8,128)(2,1)} %k_ref.1, bf16[512,512]{1,0:T(8,128)(2,1)} %v_ref.1, f32[1,4096]{1,0:T(1,128)} %bitcast.3, s32[8,32]{1,0:T(8,128)} %bitcast.4, ...), custom_call_target="tpu_custom_call" | custom-call | tf_op jit(solution)/shard_map/decoder_layer/pallas_call | solution.py:437
  77.4 1.7 %copy.17 = bf16[32,4096]{1,0:T(8,128)(2,1)} copy(bf16[32,4096]{1,0:T(8,128)(2,1)} %get-tuple-element.4) | data formatting | bytes 524288
  79.0 1.7 %copy.18 = bf16[32,4096]{1,0:T(8,128)(2,1)} copy(bf16[32,4096]{1,0:T(8,128)(2,1)} %get-tuple-element.5) | data formatting | bytes 524288
where the time goes:
time: 80.9 us; the launch traced here: 80.7 us
  Pallas kernels  76.1 us (94%)
  local copies, waits for them, and re-layouts  3.34 us (4%)
  between operations  1.29 us (2%)
    pallas_call x1, Pallas kernels, on_device_fused(): pl.pallas_call(fused_kernel, out_shape=(jax.ShapeDtypeStruct((ROWS, D), b...  76.1 us
    unnamed x2, local copies, waits for them, and re-layouts  3.34 us

commit v1 on v0

--- a/solution.py
+++ b/solution.py
@@ -97,7 +97,8 @@
     kv = (me * (HEAD_COLS // HEAD_DIM)) // (HEADS // KV_HEADS)
     kv_cols = pl.ds(pl.multiple_of(kv * HEAD_DIM, HEAD_DIM), HEAD_DIM)
     scale = HEAD_DIM ** (-0.5)
-    for block in range(SEQ // QBLOCK):
+
+    def attend(block):
         first = block * QBLOCK
         keys_seen = first + QBLOCK
         q_pos = first + lax.broadcasted_iota(jnp.int32, (QBLOCK, keys_seen), 0)
@@ -125,32 +126,29 @@
             )
             attended[first : first + QBLOCK, cols] = (summed / total).astype(jnp.bfloat16)
 
-    loads[0].wait()
-    pl.semaphore_wait(barrier, N_EXP - 1)
-
     x_peer, y_peer = me + 1 - 2 * x, me + 2 - 4 * y
 
     def places(odd):
         return (y, x, y_peer, x_peer) if odd else (x, y, x_peer, y_peer)
 
-    def copy1(chunk, odd):
+    def copy1(chunk, odd, half):
         a, _, peer, _ = places(odd)
         return pltpu.make_async_remote_copy(
-            src_ref=part.at[chunk, 1 - a],
-            dst_ref=got1.at[chunk],
-            send_sem=send1.at[chunk],
-            recv_sem=recv1.at[chunk],
+            src_ref=part.at[chunk, 1 - a, half],
+            dst_ref=got1.at[chunk, half],
+            send_sem=send1.at[chunk, half],
+            recv_sem=recv1.at[chunk, half],
             device_id={"exp": peer},
             device_id_type=pl.DeviceIdType.MESH,
         )
 
-    def copy2(chunk, odd):
+    def copy2(chunk, odd, half):
         a, b, _, peer = places(odd)
         return pltpu.make_async_remote_copy(
-            src_ref=part.at[chunk, a, 1 - b],
-            dst_ref=got2.at[chunk],
-            send_sem=send2.at[chunk],
-            recv_sem=recv2.at[chunk],
+            src_ref=part.at[chunk, a, half, 1 - b],
+            dst_ref=got2.at[chunk, half],
+            send_sem=send2.at[chunk, half],
+            recv_sem=recv2.at[chunk, half],
             device_id={"exp": peer},
             device_id_type=pl.DeviceIdType.MESH,
         )
@@ -159,7 +157,7 @@
         a, b, _, _ = places(odd)
         other = (z + step) % 4
         return pltpu.make_async_remote_copy(
-            src_ref=part.at[chunk, a, b, other],
+            src_ref=part.at[chunk, a, other // 2, b, other % 2],
             dst_ref=got3.at[chunk, step - 1],
             send_sem=send3.at[chunk, step - 1],
             recv_sem=recv3.at[chunk, step - 1],
@@ -167,46 +165,54 @@
             device_id_type=pl.DeviceIdType.MESH,
         )
 
-    def project(pair):
+    def project(pair, half):
+        lines = SEQ // 2
         for odd in (0, 1):
             chunk = pair * 2 + odd
             cols = slice(chunk * WIDE, (chunk + 1) * WIDE)
-            for half in range(2):
-                lines = SEQ // 2
-                product = jnp.dot(
-                    attended[half * lines : (half + 1) * lines, :],
-                    proj[:, cols],
-                    preferred_element_type=jnp.float32,
-                ).astype(jnp.bfloat16)
-                for local in range(N_EXP // 2):
-                    owner = half * (N_EXP // 2) + local
-                    ox, oy, oz = owner % 2, (owner // 2) % 2, owner // 4
-                    a, b = (oy, ox) if odd else (ox, oy)
-                    part[chunk, a, b, oz] = product[local * ROWS : (local + 1) * ROWS, :]
-            copy1(chunk, odd).start()
-
-    def fold1(pair):
+            product = jnp.dot(
+                attended[half * lines : (half + 1) * lines, :],
+                proj[:, cols],
+                preferred_element_type=jnp.float32,
+            ).astype(jnp.bfloat16)
+            for local in range(N_EXP // 2):
+                ox, oy, oz = local % 2, (local // 2) % 2, local // 4
+                a, b = (oy, ox) if odd else (ox, oy)
+                part[chunk, a, half, b, oz] = product[local * ROWS : (local + 1) * ROWS, :]
+            copy1(chunk, odd, half).start()
+
+    def fold1(pair, half):
         for odd in (0, 1):
             chunk = pair * 2 + odd
-            a = places(odd)[0]
-            copy1(chunk, odd).wait_recv()
-            for b in range(2):
-                for c in range(4):
-                    part[chunk, a, b, c] = part[chunk, a, b, c] + got1[chunk, b, c]
-            copy2(chunk, odd).start()
+            a, b, _, _ = places(odd)
+            copy1(chunk, odd, half).wait_recv()
+            for c in range(2):
+                part[chunk, a, half, 1 - b, c] = (
+                    part[chunk, a, half, 1 - b, c] + got1[chunk, half, 1 - b, c]
+                )
+            copy2(chunk, odd, half).start()
+            for c in range(2):
+                part[chunk, a, half, b, c] = part[chunk, a, half, b, c] + got1[chunk, half, b, c]
 
     def fold2(pair):
         for odd in (0, 1):
             chunk = pair * 2 + odd
             a, b, _, _ = places(odd)
-            copy2(chunk, odd).wait_recv()
-            for c in range(4):
-                part[chunk, a, b, c] = part[chunk, a, b, c] + got2[chunk, c]
+            for half in range(2):
+                copy2(chunk, odd, half).wait_recv()
+                for c in range(2):
+                    part[chunk, a, half, b, c] = part[chunk, a, half, b, c] + got2[chunk, half, c]
             for step in range(1, 4):
                 copy3(chunk, odd, step).start()
 
-    project(0)
-    project(1)
+    attend(0)
+    loads[0].wait()
+    pl.semaphore_wait(barrier, N_EXP - 1)
+    for pair in range(CHUNKS // 2):
+        project(pair, 0)
+    attend(1)
+    project(0, 1)
+    project(1, 1)
 
     slot = lax.broadcasted_iota(jnp.int32, (SLOTS, ROWS), 0)
     row = lax.broadcasted_iota(jnp.int32, (SLOTS, ROWS), 1)
@@ -290,7 +296,7 @@
             for step in range(1, 4):
                 copy3(chunk, odd, step).wait_recv()
             cols = slice(chunk * WIDE, (chunk + 1) * WIDE)
-            total = part[chunk, a, b, z].astype(jnp.float32)
+            total = part[chunk, a, z // 2, b, z % 2].astype(jnp.float32)
             for step in range(3):
                 total = total + got3[chunk, step].astype(jnp.float32)
             total = total + hidden_ref[:, cols].astype(jnp.float32)
@@ -346,17 +352,21 @@
                 term = jnp.dot(tokens, weights_in[deep, cols], preferred_element_type=jnp.float32)
                 sums[:, cols] = term if pair == 0 else sums[:, cols] + term
 
-    fold1(0)
-    project(2)
-    fold1(1)
+    fold1(0, 0)
+    fold1(1, 0)
+    project(2, 1)
+    fold1(0, 1)
+    fold1(2, 0)
+    project(3, 1)
     fold2(0)
-    project(3)
-    fold1(2)
+    fold1(1, 1)
+    fold1(3, 0)
     fold2(1)
     final(0)
-    fold1(3)
+    fold1(2, 1)
     fold2(2)
     final(1)
+    fold1(3, 1)
     expert_in(0)
     fold2(3)
     final(2)
@@ -400,8 +410,9 @@
     def finish(pair, _):
         for odd in (0, 1):
             chunk = pair * 2 + odd
-            copy1(chunk, odd).wait_send()
-            copy2(chunk, odd).wait_send()
+            for half in range(2):
+                copy1(chunk, odd, half).wait_send()
+                copy2(chunk, odd, half).wait_send()
             for step in range(1, 4):
                 copy3(chunk, odd, step).wait_send()
         each_step(lambda step: there(pair, step).wait_send())
@@ -436,7 +447,7 @@
     norm_tiles = pltpu.VMEM((1, N_EXP, 8, 128), jnp.float32)
     return pl.pallas_call(
         fused_kernel,
-        out_shape=(jax.ShapeDtypeStruct((ROWS, D), bf16), jax.ShapeDtypeStruct((ROWS, D), bf16)),
+        out_shape=(pltpu.VMEM((ROWS, D), bf16), pltpu.VMEM((ROWS, D), bf16)),
         in_specs=[vmem] * 7 + [pl.BlockSpec(memory_space=pltpu.SMEM)] + [hbm] * 4,
         out_specs=(vmem, vmem),
         scratch_shapes=[
@@ -445,9 +456,9 @@
             pltpu.VMEM((D, FF), bf16),
             pltpu.VMEM((FF, D), bf16),
             pltpu.VMEM((SEQ, HEAD_COLS), bf16),
-            pltpu.VMEM((CHUNKS, 2, 2, 4, ROWS, WIDE), bf16),
-            pltpu.VMEM((CHUNKS, 2, 4, ROWS, WIDE), bf16),
-            pltpu.VMEM((CHUNKS, 4, ROWS, WIDE), bf16),
+            pltpu.VMEM((CHUNKS, 2, 2, 2, 2, ROWS, WIDE), bf16),
+            pltpu.VMEM((CHUNKS, 2, 2, 2, ROWS, WIDE), bf16),
+            pltpu.VMEM((CHUNKS, 2, 2, ROWS, WIDE), bf16),
             pltpu.VMEM((CHUNKS, 3, ROWS, WIDE), bf16),
             pltpu.VMEM((SLOTS, FF), jnp.float32),
             pltpu.VMEM((SLOTS, FF), jnp.float32),
@@ -459,10 +470,10 @@
             norm_tiles,
             norm_tiles,
             dma((4,)),
-            dma((CHUNKS,)),
-            dma((CHUNKS,)),
-            dma((CHUNKS,)),
-            dma((CHUNKS,)),
+            dma((CHUNKS, 2)),
+            dma((CHUNKS, 2)),
+            dma((CHUNKS, 2)),
+            dma((CHUNKS, 2)),
             dma((CHUNKS, 3)),
             dma((CHUNKS, 3)),
             dma((D // PAIR, N_EXP - 1)),

time: 80.9 us -> 83 us (1.026)
  Pallas kernels: 76.1 us -> 80.1 us
  local copies, waits for them, and re-layouts: 3.34 us -> 1.41 us
    pallas_call x1, Pallas kernels: 76.1 us -> 80.1 us  [on_device_fused(): pl.pallas_call(fused_kernel, out_shape=(pltpu.VMEM((ROWS, D), bf16), pltp...]
    unnamed x2, local copies, waits for them, and re-layouts: 3.34 us -> 1.41 us
where the time goes in v1:
time: 83 us; the launch traced here: 82.8 us
  Pallas kernels  80.1 us (97%)
  local copies, waits for them, and re-layouts  1.41 us (2%)
  between operations  1.29 us (2%)
    pallas_call x1, Pallas kernels, on_device_fused(): pl.pallas_call(fused_kernel, out_shape=(pltpu.VMEM((ROWS, D), bf16), pltp...  80.1 us

profile of v1, /device:TPU:0, one launch (start us, length us, event | category | flops | bytes accessed | tf_op | source)
XLA Modules:
  0.0 82.8 jit_solution(15854510716881605607)
XLA Ops:
  1.3 80.1 %decoder_layer.1 = (bf16[32,4096]{1,0:T(8,128)(2,1)S(1)}, bf16[32,4096]{1,0:T(8,128)(2,1)S(1)}) custom-call(bf16[32,4096]{1,0:T(8,128)(2,1)} %hidden_ref.1, bf16[512,512]{1,0:T(8,128)(2,1)} %q_ref.1, bf16[512,512]{1,0:T(8,128)(2,1)} %k_ref.1, bf16[512,512]{1,0:T(8,128)(2,1)} %v_ref.1, f32[1,4096]{1,0:T(1,128)} %bitcast.3, s32[8,32]{1,0:T(8,128)} %bitcast.4, ...), custom_call_target="tpu_custom_call" | custom-call | tf_op jit(solution)/shard_map/decoder_layer/pallas_call | solution.py:448
  81.4 0.7 copy.16
  82.1 0.7 copy.17
